TPU v7x, 128 devices: a whole 4x4x4 slice. The times are simulated.
128 devices in a mesh: rep: 16 (over x_lo, z, core), shard: 8 (over x_hi, y).
Axes of the slice: x: 4 (x_hi: 2, x_lo: 2; x = x_hi * 2 + x_lo), y: 4, z: 4, core: 2. Of those that a mesh axis runs over, the one named last changes fastest.
Arguments:
- latents: bfloat16 [16, 1024, 1024], P('rep', 'shard'), may hold values from -6 to 6
- cond: bfloat16 [16, 1024], P('rep'), may hold values from -6 to 6
- cotangent: bfloat16 [16, 1024, 1024], P('rep', 'shard'), may hold values from -6 to 6
- w_qkv: bfloat16 [1024, 3072], P('shard'), may hold values from -0.1875 to 0.1875
- bias_qv: bfloat16 [2048], P('shard'), may hold values from -3 to 3
- w_proj: bfloat16 [1024, 1024], P('shard'), may hold values from -1 to 1
- b_proj: bfloat16 [1024], P('shard'), may hold values from -3 to 3
- w_fc1: bfloat16 [1024, 4096], P('shard'), may hold values from -0.1875 to 0.1875
- b_fc1: bfloat16 [4096], P('shard'), may hold values from -3 to 3
- w_fc2: bfloat16 [4096, 1024], P('shard'), may hold values from -0.09375 to 0.09375
- b_fc2: bfloat16 [1024], P('shard'), may hold values from -3 to 3
- w_ada: bfloat16 [1024, 6144], P('shard'), may hold values from -0.1875 to 0.1875
- b_ada: bfloat16 [6144], P('shard'), may hold values from -3 to 3
Outputs:
- output: bfloat16 [16, 1024, 1024], P('rep', 'shard')
- grad_latents: bfloat16 [16, 1024, 1024], P('rep', 'shard')
- grad_cond: float32 [16, 1024], P('rep')
- grad_w_qkv: float32 [1024, 3072], P('shard')
- grad_bias_qv: float32 [2048], P('shard')
- grad_w_proj: float32 [1024, 1024], P('shard')
- grad_b_proj: float32 [1024], P('shard')
- grad_w_fc1: float32 [1024, 4096], P('shard')
- grad_b_fc1: float32 [4096], P('shard')
- grad_w_fc2: float32 [4096, 1024], P('shard')
- grad_b_fc2: float32 [1024], P('shard')
- grad_w_ada: float32 [1024, 6144], P('shard')
- grad_b_ada: float32 [6144], P('shard')
All inputs are finite; a program needn't handle non-finite values.
Results may differ from a plain program's by a relative error of at most 0.025.
Values may be sent and summed in bfloat16 or wider, within the bound.
No kernel may reach another device: no remote copies, remote signals or barrier semaphores. Data moves between devices by JAX's collectives and lax.ppermute only.
A program may use at most 192 MiB of HBM per device.

v0:
```python
import jax
import jax.numpy as jnp
from jax import lax
from jax.sharding import PartitionSpec as P

HEAD = 64
epsilon = 1e-06
highest = lax.Precision.HIGHEST


def as_sent(value):
    return jax.tree.map(lambda a: a.astype(jnp.bfloat16) if a.dtype == jnp.float32 else a, value)


def layer_norm(values):
    centered = values - jnp.mean(values, axis=-1, keepdims=True)
    variance = jnp.mean(centered * centered, axis=-1, keepdims=True)
    return centered * lax.rsqrt(variance + epsilon)


def sigmoid_linear(values):
    return values / (1.0 + jnp.exp(-values))


def gelu_tanh(values):
    return (
        0.5
        * values
        * (1.0 + jnp.tanh(0.7978845608028654 * (values + 0.044715 * values * values * values)))
    )


def project(left, right):
    return jnp.einsum("lrd,de->lre", left, right, preferred_element_type=jnp.float32)


def project_back(left, right):
    return jnp.einsum("lre,de->lrd", left, right, preferred_element_type=jnp.float32)


def on_device(
    latents,
    cond,
    cotangent,
    w_qkv,
    bias_qv,
    w_proj,
    b_proj,
    w_fc1,
    b_fc1,
    w_fc2,
    b_fc2,
    w_ada,
    b_ada,
):
    count_lat = latents.shape[0]
    rows = latents.shape[1]
    features = latents.shape[2]
    heads = features // HEAD
    score_scale = HEAD ** (-0.5)
    gathered = (
        lax.all_gather(w_qkv, "shard", axis=0, tiled=True),
        lax.all_gather(bias_qv, "shard", axis=0, tiled=True),
        lax.all_gather(w_proj, "shard", axis=0, tiled=True),
        lax.all_gather(b_proj, "shard", axis=0, tiled=True),
        lax.all_gather(w_fc1, "shard", axis=0, tiled=True),
        lax.all_gather(b_fc1, "shard", axis=0, tiled=True),
        lax.all_gather(w_fc2, "shard", axis=0, tiled=True),
        lax.all_gather(b_fc2, "shard", axis=0, tiled=True),
        lax.all_gather(w_ada, "shard", axis=0, tiled=True),
        lax.all_gather(b_ada, "shard", axis=0, tiled=True),
    )
    whole_qkv = gathered[0]
    whole_proj = gathered[2]
    whole_fc1 = gathered[4]
    whole_fc2 = gathered[6]
    whole_ada = gathered[8]
    bias_wide = gathered[1].astype(jnp.float32)
    stream = latents.astype(jnp.float32)
    cond_value = cond.astype(jnp.float32)
    cond_silu, silu_pull = jax.vjp(sigmoid_linear, cond_value)
    cond_low = cond_silu.astype(jnp.bfloat16)
    modulation = jnp.dot(cond_low, whole_ada, preferred_element_type=jnp.float32) + gathered[
        9
    ].astype(jnp.float32)
    shift_first, scale_first, gate_first, shift_second, scale_second, gate_second = jnp.split(
        modulation[:, None, :], 6, axis=2
    )
    norm_first, first_pull = jax.vjp(layer_norm, stream)
    attend_in = (norm_first * (1.0 + scale_first) + shift_first).astype(jnp.bfloat16)
    packed = project(attend_in, whole_qkv)
    queries = (packed[:, :, :features] + bias_wide[:features]).astype(jnp.bfloat16)
    keyset = packed[:, :, features : 2 * features].astype(jnp.bfloat16)
    valueset = (packed[:, :, 2 * features :] + bias_wide[features:]).astype(jnp.bfloat16)
    key_all, value_all = (
        lax.all_gather(keyset, "shard", axis=1, tiled=True),
        lax.all_gather(valueset, "shard", axis=1, tiled=True),
    )
    length = key_all.shape[1]
    query_heads = queries.reshape(count_lat, rows, heads, HEAD)
    key_heads = key_all.reshape(count_lat, length, heads, HEAD)
    value_heads = value_all.reshape(count_lat, length, heads, HEAD)
    scores = (
        jnp.einsum("lqhe,lkhe->lhqk", query_heads, key_heads, preferred_element_type=jnp.float32)
        * score_scale
    )
    row_peak = jnp.max(scores, axis=-1, keepdims=True)
    powered = jnp.exp(scores - row_peak)
    row_total = jnp.sum(powered, axis=-1, keepdims=True)
    attention = powered / row_total
    log_total = row_peak + jnp.log(row_total)
    mixed_heads = jnp.einsum(
        "lhqk,lkhe->lqhe",
        attention.astype(jnp.bfloat16),
        value_heads,
        preferred_element_type=jnp.float32,
    )
    mixed_low = mixed_heads.reshape(count_lat, rows, features).astype(jnp.bfloat16)
    branch = project(mixed_low, whole_proj) + gathered[3].astype(jnp.float32)
    middle = stream + gate_first * branch
    norm_second, second_pull = jax.vjp(layer_norm, middle)
    feed_in = (norm_second * (1.0 + scale_second) + shift_second).astype(jnp.bfloat16)
    hidden = project(feed_in, whole_fc1) + gathered[5].astype(jnp.float32)
    active_value, gelu_pull = jax.vjp(gelu_tanh, hidden)
    active_low = active_value.astype(jnp.bfloat16)
    branch_second = project(active_low, whole_fc2) + gathered[7].astype(jnp.float32)
    output = (middle + gate_second * branch_second).astype(jnp.bfloat16)
    regathered = (
        lax.all_gather(w_qkv, "shard", axis=0, tiled=True),
        lax.all_gather(w_proj, "shard", axis=0, tiled=True),
        lax.all_gather(w_fc1, "shard", axis=0, tiled=True),
        lax.all_gather(w_fc2, "shard", axis=0, tiled=True),
        lax.all_gather(w_ada, "shard", axis=0, tiled=True),
    )
    back_qkv = regathered[0]
    back_proj = regathered[1]
    back_fc1 = regathered[2]
    back_fc2 = regathered[3]
    back_ada = regathered[4]
    upstream = cotangent.astype(jnp.float32)
    grad_gate_second = jnp.sum(upstream * branch_second, axis=1)
    grad_branch_second = (upstream * gate_second).astype(jnp.bfloat16)
    grad_active = project_back(grad_branch_second, back_fc2)
    grad_hidden = gelu_pull(grad_active)[0].astype(jnp.bfloat16)
    grad_feed = project_back(grad_hidden, back_fc1)
    grad_scale_second = jnp.sum(grad_feed * norm_second, axis=1)
    grad_shift_second = jnp.sum(grad_feed, axis=1)
    grad_middle = upstream + second_pull(grad_feed * (1.0 + scale_second))[0]
    grad_gate_first = jnp.sum(grad_middle * branch, axis=1)
    grad_branch = (grad_middle * gate_first).astype(jnp.bfloat16)
    grad_mixed = (
        project_back(grad_branch, back_proj)
        .astype(jnp.bfloat16)
        .reshape(count_lat, rows, heads, HEAD)
    )
    again_scores = (
        jnp.einsum("lqhe,lkhe->lhqk", query_heads, key_heads, preferred_element_type=jnp.float32)
        * score_scale
    )
    again_probs = jnp.exp(again_scores - log_total)
    grad_probs = jnp.einsum(
        "lqhe,lkhe->lhqk", grad_mixed, value_heads, preferred_element_type=jnp.float32
    )
    grad_value = jnp.einsum(
        "lhqk,lqhe->lkhe",
        again_probs.astype(jnp.bfloat16),
        grad_mixed,
        preferred_element_type=jnp.float32,
    )
    row_delta = jnp.sum(again_probs * grad_probs, axis=-1, keepdims=True)
    grad_scores = (again_probs * (grad_probs - row_delta)).astype(jnp.bfloat16)
    grad_query = (
        (
            jnp.einsum(
                "lhqk,lkhe->lqhe", grad_scores, key_heads, preferred_element_type=jnp.float32
            )
            * score_scale
        )
        .reshape(count_lat, rows, features)
        .astype(jnp.bfloat16)
    )
    grad_key = (
        jnp.einsum("lhqk,lqhe->lkhe", grad_scores, query_heads, preferred_element_type=jnp.float32)
        * score_scale
    )
    key_owned, value_owned = (
        lax.psum_scatter(
            grad_key.reshape(count_lat, length, features).astype(jnp.bfloat16),
            "shard",
            scatter_dimension=1,
            tiled=True,
        ).astype(jnp.float32),
        lax.psum_scatter(
            grad_value.reshape(count_lat, length, features).astype(jnp.bfloat16),
            "shard",
            scatter_dimension=1,
            tiled=True,
        ).astype(jnp.float32),
    )
    key_low = key_owned.astype(jnp.bfloat16)
    value_low = value_owned.astype(jnp.bfloat16)
    grad_packed = jnp.concatenate([grad_query, key_low, value_low], axis=2)
    grad_attend = project_back(grad_packed, back_qkv)
    grad_scale_first = jnp.sum(grad_attend * norm_first, axis=1)
    grad_shift_first = jnp.sum(grad_attend, axis=1)
    grad_stream = grad_middle + first_pull(grad_attend * (1.0 + scale_first))[0]
    grad_latents = grad_stream.astype(jnp.bfloat16)
    grad_modulation = jnp.concatenate(
        [
            grad_shift_first,
            grad_scale_first,
            grad_gate_first,
            grad_shift_second,
            grad_scale_second,
            grad_gate_second,
        ],
        axis=1,
    )
    cond_wide = cond_low.astype(jnp.float32)
    cond_term = jnp.einsum(
        "lm,dm->ld",
        grad_modulation,
        back_ada,
        precision=highest,
        preferred_element_type=jnp.float32,
    )
    cond_total = lax.psum(cond_term, "shard")
    grad_cond = silu_pull(cond_total)[0]
    term_qkv = jnp.einsum("lrc,lre->ce", attend_in, grad_packed, preferred_element_type=jnp.float32)
    term_proj = jnp.einsum(
        "lrc,lre->ce", mixed_low, grad_branch, preferred_element_type=jnp.float32
    )
    term_fc1 = jnp.einsum("lrc,lre->ce", feed_in, grad_hidden, preferred_element_type=jnp.float32)
    pieces = [term_qkv, term_proj, term_fc1]
    pieces.append(jnp.dot(cond_wide.T, grad_modulation, precision=highest))
    row_owned = lax.psum_scatter(
        jnp.concatenate(pieces, axis=1).astype(jnp.bfloat16),
        "shard",
        scatter_dimension=0,
        tiled=True,
    ).astype(jnp.float32)
    units = active_low.shape[2]
    second_owned = lax.psum_scatter(
        jnp.einsum(
            "lrc,lre->ce", active_low, grad_branch_second, preferred_element_type=jnp.float32
        ).astype(jnp.bfloat16),
        "shard",
        scatter_dimension=0,
        tiled=True,
    )
    bias_query = jnp.sum(grad_query.astype(jnp.float32), axis=(0, 1))
    bias_value = jnp.sum(value_low.astype(jnp.float32), axis=(0, 1))
    base_terms = (
        jnp.concatenate([bias_query, bias_value], axis=0),
        jnp.sum(grad_branch.astype(jnp.float32), axis=(0, 1)),
        jnp.sum(grad_hidden.astype(jnp.float32), axis=(0, 1)),
        jnp.sum(grad_branch_second.astype(jnp.float32), axis=(0, 1)),
    )
    bias_terms = base_terms + (jnp.sum(grad_modulation, axis=0),)
    bias_owned = jax.tree.map(
        lambda part: part.astype(jnp.float32),
        lax.psum_scatter(as_sent(bias_terms), "shard", scatter_dimension=0, tiled=True),
    )
    wide_qkv = 3 * features
    owned_qkv = row_owned[:, :wide_qkv]
    owned_proj = row_owned[:, wide_qkv : wide_qkv + features]
    owned_fc1 = row_owned[:, wide_qkv + features : wide_qkv + features + units]
    owned_ada = row_owned[:, wide_qkv + features + units :]
    owned_ada_bias = bias_owned[4]
    totals = (
        lax.psum(owned_qkv.astype(jnp.bfloat16), "rep").astype(jnp.float32),
        lax.psum(bias_owned[0].astype(jnp.bfloat16), "rep").astype(jnp.float32),
        lax.psum(owned_proj.astype(jnp.bfloat16), "rep").astype(jnp.float32),
        lax.psum(bias_owned[1].astype(jnp.bfloat16), "rep").astype(jnp.float32),
        lax.psum(owned_fc1.astype(jnp.bfloat16), "rep").astype(jnp.float32),
        lax.psum(bias_owned[2].astype(jnp.bfloat16), "rep").astype(jnp.float32),
        lax.psum(second_owned, "rep").astype(jnp.float32),
        lax.psum(bias_owned[3].astype(jnp.bfloat16), "rep").astype(jnp.float32),
        lax.psum(owned_ada.astype(jnp.bfloat16), "rep").astype(jnp.float32),
        lax.psum(owned_ada_bias.astype(jnp.bfloat16), "rep").astype(jnp.float32),
    )
    return (
        output,
        grad_latents,
        grad_cond,
        totals[0],
        totals[1],
        totals[2],
        totals[3],
        totals[4],
        totals[5],
        totals[6],
        totals[7],
        totals[8],
        totals[9],
    )


def solution(mesh):
    placed = (
        P("rep", "shard", None),
        P("rep", None),
        P("rep", "shard", None),
        P("shard", None),
        P("shard"),
        P("shard", None),
        P("shard"),
        P("shard", None),
        P("shard"),
        P("shard", None),
        P("shard"),
        P("shard", None),
        P("shard"),
    )
    return jax.shard_map(
        on_device,
        mesh=mesh,
        in_specs=placed,
        out_specs=(
            P("rep", "shard", None),
            P("rep", "shard", None),
            P("rep", None),
            P("shard", None),
            P("shard"),
            P("shard", None),
            P("shard"),
            P("shard", None),
            P("shard"),
            P("shard", None),
            P("shard"),
            P("shard", None),
            P("shard"),
        ),
        check_vma=False,
    )
```

profile of v0, /device:TPU:0, one launch (start us, length us, event | category | flops | bytes accessed | tf_op | source)
XLA Modules:
  0.0 1435.8 jit_solution(15415909941565255366)
XLA Ops:
  10.1 34.8 %all-gather = bf16[8,1,768]{2,1,0:T(2,128)(2,1)S(1)} all-gather(bf16[1,1,768]{2,1,0:T(2,128)(2,1)S(1)} %reshape.411), channel_id=1, replica_groups=mesh['rep'=16,'shard'=8] {'shard'}, dimensions={0}, use_global_device_ids=true | all-gather | bytes 13824 | tf_op jit(solution)/shard_map/all_gather | solution.py:71
  44.8 22.8 %all-gather.1 = bf16[8,1,256]{2,1,0:T(2,128)(2,1)S(1)} all-gather(bf16[1,1,256]{2,1,0:T(2,128)(2,1)S(1)} %reshape.413), channel_id=1, replica_groups=mesh['rep'=16,'shard'=8] {'shard'}, dimensions={0}, use_global_device_ids=true | all-gather | bytes 4608 | tf_op jit(solution)/shard_map/all_gather | solution.py:63
  70.0 87.9 %all-gather.13.cloned.1.call-done = bf16[1024,6144]{1,0:T(8,128)(2,1)} async-done(((bf16[128,6144]{1,0:T(8,128)(2,1)}), bf16[1024,6144]{1,0:T(8,128)(2,1)}) %all-gather.13.cloned.1.call-update) | async-done | bytes 12582928 | tf_op jit(solution)/shard_map/all_gather | solution.py:70
  157.9 6.3 fusion.53
  164.2 82.7 %all-gather.15.cloned.1.call-done = bf16[1024,3072]{1,0:T(8,128)(2,1)} async-done(((bf16[128,3072]{1,0:T(8,128)(2,1)}), bf16[1024,3072]{1,0:T(8,128)(2,1)}) %all-gather.15.cloned.1.call-update) | async-done | bytes 6291472 | tf_op jit(solution)/shard_map/all_gather | solution.py:62
  254.4 18.8 %all-gather.2 = bf16[8,1,128]{2,1,0:T(2,128)(2,1)S(1)} all-gather(bf16[1,1,128]{2,1,0:T(2,128)(2,1)S(1)} %bitcast.211), channel_id=1, replica_groups=mesh['rep'=16,'shard'=8] {'shard'}, dimensions={0}, use_global_device_ids=true | all-gather | bytes 2304 | tf_op jit(solution)/shard_map/all_gather | solution.py:65
  273.3 29.7 %all-gather.3 = bf16[8,1,512]{2,1,0:T(2,128)(2,1)S(1)} all-gather(bf16[1,1,512]{2,1,0:T(2,128)(2,1)S(1)} %reshape.417), channel_id=1, replica_groups=mesh['rep'=16,'shard'=8] {'shard'}, dimensions={0}, use_global_device_ids=true | all-gather | bytes 9216 | tf_op jit(solution)/shard_map/all_gather | solution.py:67
  307.7 50.6 %all-gather.19.cloned.1.call-done = bf16[1,1024,1024]{2,1,0:T(8,128)(2,1)} async-done(((bf16[1,128,1024]{2,1,0:T(8,128)(2,1)}), bf16[1,1024,1024]{2,1,0:T(8,128)(2,1)}) %all-gather.19.cloned.1.call-update) | async-done | bytes 2097168 | tf_op jit(solution)/shard_map/all_gather | solution.py:96
  369.0 43.3 %all-gather.21.cloned.1.call-done = bf16[1024,1024]{1,0:T(8,128)(2,1)} async-done(((bf16[128,1024]{1,0:T(8,128)(2,1)}), bf16[1024,1024]{1,0:T(8,128)(2,1)}) %all-gather.21.cloned.1.call-update) | async-done | bytes 2097168 | tf_op jit(solution)/shard_map/all_gather | solution.py:64
  415.5 104.0 %all-gather.23.cloned.1.call-done = bf16[1024,4096]{1,0:T(8,128)(2,1)} async-done(((bf16[128,4096]{1,0:T(8,128)(2,1)}), bf16[1024,4096]{1,0:T(8,128)(2,1)}) %all-gather.23.cloned.1.call-update) | async-done | bytes 8388624 | tf_op jit(solution)/shard_map/all_gather | solution.py:66
  519.5 6.1 convolution_add_fusion
  525.6 101.2 %all-gather.25.cloned.1.call-done = bf16[4096,1024]{1,0:T(8,128)(2,1)} async-done(((bf16[512,1024]{1,0:T(8,128)(2,1)}), bf16[4096,1024]{1,0:T(8,128)(2,1)}) %all-gather.25.cloned.1.call-update) | async-done | bytes 8388624 | tf_op jit(solution)/shard_map/all_gather | solution.py:68
  626.8 8.3 fusion.74
  643.4 6.7 fusion.13
  650.1 10.9 copy.47
  665.5 6.8 multiply_reduce_fusion
  681.0 11.0 copy.45
  696.4 18.8 %all-gather.4 = bf16[8,1,128]{2,1,0:T(2,128)(2,1)S(1)} all-gather(bf16[1,1,128]{2,1,0:T(2,128)(2,1)S(1)} %bitcast.212), channel_id=1, replica_groups=mesh['rep'=16,'shard'=8] {'shard'}, dimensions={0}, use_global_device_ids=true | all-gather | bytes 2304 | tf_op jit(solution)/shard_map/all_gather | solution.py:69
  726.4 5.7 convolution_convert_fusion.1
  732.1 6.2 reduce-scatter.15.cloned.1.call-done
  740.3 76.1 %reduce-scatter.13.cloned.1.call-done = bf16[128,1024]{1,0:T(8,128)(2,1)} async-done(((bf16[1024,1024]{1,0:T(8,128)(2,1)}), bf16[128,1024]{1,0:T(8,128)(2,1)}) %reduce-scatter.13.cloned.1.call-update) | async-done | bytes 262160
  823.6 6.2 fusion.28
  832.2 6.2 fusion.30
  838.5 7.5 multiply_convert_fusion
  846.0 19.0 %pad_maximum_fusion = bf16[1024,14336]{1,0:T(8,128)(2,1)} fusion(bf16[1024,6144]{1,0:T(8,128)(2,1)} %multiply_convert_fusion, bf16[1024,4096]{1,0:T(8,128)(2,1)} %convolution_convert_fusion.1, bf16[1024,1024]{1,0:T(8,128)(2,1)S(1)} %copy-done.5, bf16[1024,3072]{1,0:T(8,128)(2,1)} %convolution_convert_fusion.2), kind=kLoop, calls=%fused_computation | loop fusion | flops 117440512 | bytes 58720256 | tf_op jit(solution)/shard_map/concatenate | solution.py:237
  871.6 294.5 %reduce-scatter.9.cloned.1.call-done = bf16[128,14336]{1,0:T(8,128)(2,1)} async-done(((bf16[1024,14336]{1,0:T(8,128)(2,1)}), bf16[128,14336]{1,0:T(8,128)(2,1)}) %reduce-scatter.9.cloned.1.call-update) | async-done | bytes 3670032 | tf_op jit(solution)/shard_map/reduce_scatter | solution.py:236
  1174.9 108.2 %reduce-scatter.11.cloned.1.call-done = bf16[512,1024]{1,0:T(8,128)(2,1)} async-done(((bf16[4096,1024]{1,0:T(8,128)(2,1)}), bf16[512,1024]{1,0:T(8,128)(2,1)}) %reduce-scatter.11.cloned.1.call-update) | async-done | bytes 1048592 | tf_op jit(solution)/shard_map/reduce_scatter | solution.py:243
  1286.4 38.0 %all-reduce.7 = (bf16[2048]{0:T(1024)(128)(2,1)S(1)}, bf16[1024]{0:T(1024)(128)(2,1)S(1)}, bf16[4096]{0:T(1024)(128)(2,1)S(1)}, bf16[1024]{0:T(1024)(128)(2,1)S(1)}, bf16[6144]{0:T(1024)(128)(2,1)S(1)}) all-reduce(bf16[2048]{0:T(1024)(128)(2,1)S(1)} %pad_maximum_fusion.1, ...), channel_id=5, replica_groups=mesh['rep'=16,'shard'=8] {'shard'}, use_global_device_ids=true, to_apply=%region_24.0.clone | all-reduce | flops 14336 | bytes 57344
  1324.8 27.9 %all-reduce.5 = (bf16[256]{0:T(256)(128)(2,1)S(1)}, bf16[128]{0:T(256)(128)(2,1)S(1)}, bf16[512]{0:T(512)(128)(2,1)S(1)}, bf16[128]{0:T(256)(128)(2,1)S(1)}, bf16[768]{0:T(1024)(128)(2,1)S(1)}) all-reduce(bf16[256]{0:T(256)(128)(2,1)S(1)} %dynamic-slice.1, ...), channel_id=1, replica_groups=mesh['rep'=16,'shard'=8] {'rep'}, use_global_device_ids=true, to_apply=%region_25.0 | all-reduce | flops 1792 | bytes 7168 | tf_op jit(solution)/shard_map/psum | solution.py:272
  1355.5 12.7 fusion.50
  1368.2 19.0 %psum.77 = f32[1,1024]{1,0:T(1,128)S(1)} all-reduce(f32[1,1024]{1,0:T(1,128)S(1)} %fusion.50), channel_id=1, replica_groups=mesh['rep'=16,'shard'=8] {'shard'}, use_global_device_ids=true, to_apply=%region_19.0 | all-reduce | flops 1024 | bytes 8192 | tf_op jit(solution)/shard_map/psum | solution.py:227
  1387.8 30.2 %all-reduce.10.cloned.1.call-done = (bf16[128,3072]{1,0:T(8,128)(2,1)}, bf16[128,1024]{1,0:T(8,128)(2,1)}, bf16[128,4096]{1,0:T(8,128)(2,1)}, bf16[512,1024]{1,0:T(8,128)(2,1)}, bf16[128,6144]{1,0:T(8,128)(2,1)}) async-done(((bf16[128,3072]{1,0:T(8,128)(2,1)}, bf16[128,1024]{1,0:T(8,128)(2,1)}, bf16[128,4096]{1,0:T(8,128)(2,1)}, bf16[512,1024]{1,0:T(8,128)(2,1)}, bf16[128,6144]{1,0:T(8,128)(2,1)}), ...) | async-done | bytes 4718608 | tf_op jit(solution)/shard_map/psum | solution.py:271
  (168 shorter events, 110.4 us)
Async XLA Ops:
  7.2 150.7 %all-gather.13.cloned.1.call-start = ((), (), s32[]{:S(2)}) async-start(), calls=%async_computation.4 | async-start | bytes 14155776 | tf_op jit(solution)/shard_map/all_gather | solution.py:70
  7.9 239.0 %all-gather.15.cloned.1.call-start = ((), (), s32[]{:S(2)}) async-start(), calls=%async_computation.5 | async-start | bytes 7077888 | tf_op jit(solution)/shard_map/all_gather | solution.py:62
  8.7 295.1 %all-gather.17.cloned.1.call-start = ((), (), s32[]{:S(2)}) async-start(), calls=%async_computation.6 | async-start | bytes 2359296 | tf_op jit(solution)/shard_map/all_gather | solution.py:97
  70.0 176.9 %copy-start.3 = (bf16[1,128,1024]{2,1,0:T(8,128)(2,1)S(1)}, bf16[1,128,1024]{2,1,0:T(8,128)(2,1)}, u32[]{:S(2)}) copy-start(bf16[1,128,1024]{2,1,0:T(8,128)(2,1)} %param.13) | copy-start | bytes 786436
  250.8 3.7 copy-start.26
  251.6 106.7 %all-gather.19.cloned.1.call-start = ((), (), s32[]{:S(2)}) async-start(), calls=%async_computation.7 | async-start | bytes 2359296 | tf_op jit(solution)/shard_map/all_gather | solution.py:96
  252.5 159.9 %all-gather.21.cloned.1.call-start = ((), (), s32[]{:S(2)}) async-start(), calls=%async_computation.8 | async-start | bytes 2359296 | tf_op jit(solution)/shard_map/all_gather | solution.py:64
  253.0 266.4 %all-gather.23.cloned.1.call-start = ((), (), s32[]{:S(2)}) async-start(), calls=%async_computation.9 | async-start | bytes 9437184 | tf_op jit(solution)/shard_map/all_gather | solution.py:66
  253.6 373.1 %all-gather.25.cloned.1.call-start = ((), (), s32[]{:S(2)}) async-start(), calls=%async_computation.10 | async-start | bytes 9437184 | tf_op jit(solution)/shard_map/all_gather | solution.py:68
  254.4 483.9 %reduce-scatter.15.cloned.1.call-start = ((), (), s32[]{:S(2)}) async-start(), calls=%async_computation.14 | async-start | bytes 2359296
  303.1 58.1 %copy-start.10 = (bf16[1,128,1024]{1,2,0:T(8,128)(2,1)}, bf16[1,128,1024]{1,2,0:T(8,128)(2,1)S(1)}, u32[]{:S(2)}) copy-start(bf16[1,128,1024]{1,2,0:T(8,128)(2,1)S(1)} %copy.41) | copy-start | bytes 786436
  369.0 150.5 %copy-start.23 = (bf16[16,64,128]{2,1,0:T(8,128)(2,1)}, bf16[16,64,128]{2,1,0:T(8,128)(2,1)S(1)}, u32[]{:S(2)}) copy-start(bf16[16,64,128]{2,1,0:T(8,128)(2,1)S(1)} %fusion.16) | copy-start | bytes 786436
  519.5 107.3 %copy-start.16 = (bf16[1,128,1024]{2,1,0:T(8,128)(2,1)S(1)}, bf16[1,128,1024]{2,1,0:T(8,128)(2,1)}, u32[]{:S(2)}) copy-start(bf16[1,128,1024]{2,1,0:T(8,128)(2,1)} %param.15) | copy-start | bytes 786436
  626.8 8.3 copy-start.1
  635.0 4.1 copy-start.17
  635.0 5.0 copy-start.6
  665.3 151.1 %reduce-scatter.13.cloned.1.call-start = ((), (), s32[]{:S(2)}) async-start(), calls=%async_computation.13 | async-start | bytes 2359296
  672.3 6.6 copy-start.11
  691.9 4.5 copy-start.24
  691.9 4.5 copy-start.27
  696.3 469.9 %reduce-scatter.9.cloned.1.call-start = ((), (), s32[]{:S(2)}) async-start(), calls=%async_computation.11 | async-start | bytes 33030144 | tf_op jit(solution)/shard_map/reduce_scatter | solution.py:236
  722.3 4.1 copy-start.9
  726.4 91.9 %copy-start.20 = (bf16[16,64,128]{2,1,0:T(8,128)(2,1)}, bf16[16,64,128]{2,1,0:T(8,128)(2,1)S(1)}, u32[]{:S(2)}) copy-start(bf16[16,64,128]{2,1,0:T(8,128)(2,1)S(1)} %get-tuple-element.64) | copy-start | bytes 786436
  740.3 78.0 %copy-start.21 = (bf16[1,128,1024]{1,2,0:T(8,128)(2,1)}, bf16[1,128,1024]{1,2,0:T(8,128)(2,1)S(1)}, u32[]{:S(2)}) copy-start(bf16[1,128,1024]{1,2,0:T(8,128)(2,1)S(1)} %copy.48) | copy-start | bytes 786436
  823.6 8.7 copy-start.4
  823.6 8.7 copy-start.14
  838.5 7.5 copy-start.5
  865.0 418.1 %reduce-scatter.11.cloned.1.call-start = ((), (), s32[]{:S(2)}) async-start(), calls=%async_computation.12 | async-start | bytes 9437184 | tf_op jit(solution)/shard_map/reduce_scatter | solution.py:243
  871.6 546.4 %all-reduce.10.cloned.1.call-start = ((), (), s32[]{:S(2)}) async-start(), calls=%async_computation.15 | async-start | bytes 9437184 | tf_op jit(solution)/shard_map/psum | solution.py:271
  1172.2 111.0 %copy-start.28 = (u32[128]{0:T(128)S(1)}, u32[128]{0:T(128)}, u32[]{:S(2)}) copy-start(u32[128]{0:T(128)} %constant.43) | copy-start | bytes 1540
  1418.0 7.2 copy-start.19
  1419.8 6.9 copy-start.15
  (9 other events, 18.9 us)
Sparse Core Ops, SparseCore 0:
  10.3 147.5 all-gather.12
  160.2 86.6 all-gather.14
  251.8 51.9 all-gather.16
  306.5 51.7 all-gather.18
  360.5 51.7 all-gather.20
  414.6 104.8 all-gather.22
  521.8 104.8 all-gather.24
  665.4 72.8 reduce-scatter.14
  742.6 73.7 reduce-scatter.12
  865.2 300.9 reduce-scatter.8
  1170.0 113.0 reduce-scatter.10
  1287.3 130.6 all-reduce.9
where the time goes:
time: 1440 us
  waiting for transfers between devices  989 us (69%)
  blocking collectives  210 us (15%)
  matrix products  99.9 us (7%)
  local copies, waits for them, and re-layouts  64.3 us (4%)
  other arithmetic  55 us (4%)
  between operations  17.5 us (1%)
    reduce_scatter x1, waiting for transfers between devices, on_device(): lax.psum_scatter(jnp.concatenate(pieces, axis=1).astype(jnp.bfloat16), 's...  295 us
    reduce_scatter x1, waiting for transfers between devices, on_device(): lax.psum_scatter(jnp.einsum('lrc,lre->ce', active_low, grad_branch_second...  108 us
    all_gather x1, waiting for transfers between devices, on_device(): lax.all_gather(w_fc1, 'shard', axis=0, tiled=True)  104 us
    all_gather x1, waiting for transfers between devices, on_device(): lax.all_gather(w_fc2, 'shard', axis=0, tiled=True)  101 us
    all_gather x1, waiting for transfers between devices, on_device(): lax.all_gather(w_ada, 'shard', axis=0, tiled=True)  87.9 us
    unnamed x14, waiting for transfers between devices  85.5 us
    all_gather x1, waiting for transfers between devices, on_device(): lax.all_gather(w_qkv, 'shard', axis=0, tiled=True)  82.7 us
    all_gather x1, waiting for transfers between devices, on_device(): lax.all_gather(keyset, 'shard', axis=1, tiled=True)  50.6 us
  transfers between devices with their start and end apart: 12, of which 12 were waited for; matrix products, arithmetic and copies ran while one was open for 8% of the time, Pallas kernels for 0%

commit v1 on v0

--- a/solution.py
+++ b/solution.py
@@ -268,7 +268,7 @@
     owned_ada = row_owned[:, wide_qkv + features + units :]
     owned_ada_bias = bias_owned[4]
     totals = (
-        lax.psum(owned_qkv.astype(jnp.bfloat16), "rep").astype(jnp.float32),
+        jnp.sum(lax.all_gather(owned_qkv.astype(jnp.bfloat16), "rep"), axis=0).astype(jnp.float32),
         lax.psum(bias_owned[0].astype(jnp.bfloat16), "rep").astype(jnp.float32),
         lax.psum(owned_proj.astype(jnp.bfloat16), "rep").astype(jnp.float32),
         lax.psum(bias_owned[1].astype(jnp.bfloat16), "rep").astype(jnp.float32),

time: 1440 us -> 1510 us (1.049)
  waiting for transfers between devices: 989 us -> 1050 us
    all_gather x0 -> x1, waiting for transfers between devices: none -> 66 us  [on_device(): lax.all_gather(owned_qkv.astype(jnp.bfloat16), 'rep')]
    unnamed x14 -> x15, waiting for transfers between devices: 85.5 us -> 85.3 us
  transfers between devices with their start and end apart: 12 -> 13, of which waited for: 12 -> 13; matrix products, arithmetic and copies ran while one was open for 8% -> 8% of each run, Pallas kernels for 0% -> 0%
where the time goes in v1:
time: 1510 us; the launch traced here: 1500 us
  waiting for transfers between devices  1050 us (70%)
  blocking collectives  209 us (14%)
  matrix products  99.7 us (7%)
  local copies, waits for them, and re-layouts  64.5 us (4%)
  other arithmetic  61.1 us (4%)
  between operations  17.2 us (1%)
    reduce_scatter x1, waiting for transfers between devices, on_device(): lax.psum_scatter(jnp.concatenate(pieces, axis=1).astype(jnp.bfloat16), 's...  294 us
    reduce_scatter x1, waiting for transfers between devices, on_device(): lax.psum_scatter(jnp.einsum('lrc,lre->ce', active_low, grad_branch_second...  111 us
    all_gather x1, waiting for transfers between devices, on_device(): lax.all_gather(w_fc1, 'shard', axis=0, tiled=True)  104 us
    all_gather x1, waiting for transfers between devices, on_device(): lax.all_gather(w_fc2, 'shard', axis=0, tiled=True)  101 us
    all_gather x1, waiting for transfers between devices, on_device(): lax.all_gather(w_ada, 'shard', axis=0, tiled=True)  87.9 us
    unnamed x15, waiting for transfers between devices  85.3 us
    all_gather x1, waiting for transfers between devices, on_device(): lax.all_gather(w_qkv, 'shard', axis=0, tiled=True)  82.7 us
    all_gather x1, waiting for transfers between devices, on_device(): lax.all_gather(owned_qkv.astype(jnp.bfloat16), 'rep')  66 us
  transfers between devices with their start and end apart: 13, of which 13 were waited for; matrix products, arithmetic and copies ran while one was open for 8% of the time, Pallas kernels for 0%

profile of v1, /device:TPU:0, one launch (start us, length us, event | category | flops | bytes accessed | tf_op | source)
XLA Modules:
  0.0 1504.1 jit_solution(5583201972996236978)
XLA Ops:
  10.1 34.8 %all-gather.1 = bf16[8,1,768]{2,1,0:T(2,128)(2,1)S(1)} all-gather(bf16[1,1,768]{2,1,0:T(2,128)(2,1)S(1)} %reshape.412), channel_id=1, replica_groups=mesh['rep'=16,'shard'=8] {'shard'}, dimensions={0}, use_global_device_ids=true | all-gather | bytes 13824 | tf_op jit(solution)/shard_map/all_gather | solution.py:71
  44.8 22.8 %all-gather.2 = bf16[8,1,256]{2,1,0:T(2,128)(2,1)S(1)} all-gather(bf16[1,1,256]{2,1,0:T(2,128)(2,1)S(1)} %reshape.414), channel_id=1, replica_groups=mesh['rep'=16,'shard'=8] {'shard'}, dimensions={0}, use_global_device_ids=true | all-gather | bytes 4608 | tf_op jit(solution)/shard_map/all_gather | solution.py:63
  70.0 87.9 %all-gather.15.cloned.1.call-done = bf16[1024,6144]{1,0:T(8,128)(2,1)} async-done(((bf16[128,6144]{1,0:T(8,128)(2,1)}), bf16[1024,6144]{1,0:T(8,128)(2,1)}) %all-gather.15.cloned.1.call-update) | async-done | bytes 12582928 | tf_op jit(solution)/shard_map/all_gather | solution.py:70
  157.9 6.3 fusion.53
  164.2 82.7 %all-gather.17.cloned.1.call-done = bf16[1024,3072]{1,0:T(8,128)(2,1)} async-done(((bf16[128,3072]{1,0:T(8,128)(2,1)}), bf16[1024,3072]{1,0:T(8,128)(2,1)}) %all-gather.17.cloned.1.call-update) | async-done | bytes 6291472 | tf_op jit(solution)/shard_map/all_gather | solution.py:62
  254.5 18.8 %all-gather.3 = bf16[8,1,128]{2,1,0:T(2,128)(2,1)S(1)} all-gather(bf16[1,1,128]{2,1,0:T(2,128)(2,1)S(1)} %bitcast.213), channel_id=1, replica_groups=mesh['rep'=16,'shard'=8] {'shard'}, dimensions={0}, use_global_device_ids=true | all-gather | bytes 2304 | tf_op jit(solution)/shard_map/all_gather | solution.py:65
  273.3 29.7 %all-gather.4 = bf16[8,1,512]{2,1,0:T(2,128)(2,1)S(1)} all-gather(bf16[1,1,512]{2,1,0:T(2,128)(2,1)S(1)} %reshape.418), channel_id=1, replica_groups=mesh['rep'=16,'shard'=8] {'shard'}, dimensions={0}, use_global_device_ids=true | all-gather | bytes 9216 | tf_op jit(solution)/shard_map/all_gather | solution.py:67
  307.7 50.6 %all-gather.21.cloned.1.call-done = bf16[1,1024,1024]{2,1,0:T(8,128)(2,1)} async-done(((bf16[1,128,1024]{2,1,0:T(8,128)(2,1)}), bf16[1,1024,1024]{2,1,0:T(8,128)(2,1)}) %all-gather.21.cloned.1.call-update) | async-done | bytes 2097168 | tf_op jit(solution)/shard_map/all_gather | solution.py:96
  368.6 43.7 %all-gather.23.cloned.1.call-done = bf16[1024,1024]{1,0:T(8,128)(2,1)} async-done(((bf16[128,1024]{1,0:T(8,128)(2,1)}), bf16[1024,1024]{1,0:T(8,128)(2,1)}) %all-gather.23.cloned.1.call-update) | async-done | bytes 2097168 | tf_op jit(solution)/shard_map/all_gather | solution.py:64
  415.5 104.0 %all-gather.25.cloned.1.call-done = bf16[1024,4096]{1,0:T(8,128)(2,1)} async-done(((bf16[128,4096]{1,0:T(8,128)(2,1)}), bf16[1024,4096]{1,0:T(8,128)(2,1)}) %all-gather.25.cloned.1.call-update) | async-done | bytes 8388624 | tf_op jit(solution)/shard_map/all_gather | solution.py:66
  519.5 6.1 convolution_add_fusion
  525.6 101.2 %all-gather.27.cloned.1.call-done = bf16[4096,1024]{1,0:T(8,128)(2,1)} async-done(((bf16[512,1024]{1,0:T(8,128)(2,1)}), bf16[4096,1024]{1,0:T(8,128)(2,1)}) %all-gather.27.cloned.1.call-update) | async-done | bytes 8388624 | tf_op jit(solution)/shard_map/all_gather | solution.py:68
  626.8 8.3 fusion.74
  643.4 6.7 fusion.13
  650.1 10.9 copy.47
  665.6 6.8 multiply_reduce_fusion
  681.0 11.0 copy.45
  696.5 18.8 %all-gather.5 = bf16[8,1,128]{2,1,0:T(2,128)(2,1)S(1)} all-gather(bf16[1,1,128]{2,1,0:T(2,128)(2,1)S(1)} %bitcast.214), channel_id=1, replica_groups=mesh['rep'=16,'shard'=8] {'shard'}, dimensions={0}, use_global_device_ids=true | all-gather | bytes 2304 | tf_op jit(solution)/shard_map/all_gather | solution.py:69
  740.3 76.0 %reduce-scatter.13.cloned.1.call-done = bf16[128,1024]{1,0:T(8,128)(2,1)} async-done(((bf16[1024,1024]{1,0:T(8,128)(2,1)}), bf16[128,1024]{1,0:T(8,128)(2,1)}) %reduce-scatter.13.cloned.1.call-update) | async-done | bytes 262160
  823.6 6.2 fusion.28
  832.3 6.2 fusion.30
  838.6 7.5 multiply_convert_fusion
  846.1 19.0 %pad_maximum_fusion = bf16[1024,14336]{1,0:T(8,128)(2,1)} fusion(bf16[1024,6144]{1,0:T(8,128)(2,1)} %multiply_convert_fusion, bf16[1024,4096]{1,0:T(8,128)(2,1)} %convolution_convert_fusion.1, bf16[1024,1024]{1,0:T(8,128)(2,1)S(1)} %copy-done.5, bf16[1024,3072]{1,0:T(8,128)(2,1)} %convolution_convert_fusion.2), kind=kLoop, calls=%fused_computation | loop fusion | flops 117440512 | bytes 58720256 | tf_op jit(solution)/shard_map/concatenate | solution.py:237
  871.7 294.2 %reduce-scatter.9.cloned.1.call-done = bf16[128,14336]{1,0:T(8,128)(2,1)} async-done(((bf16[1024,14336]{1,0:T(8,128)(2,1)}), bf16[128,14336]{1,0:T(8,128)(2,1)}) %reduce-scatter.9.cloned.1.call-update) | async-done | bytes 3670032 | tf_op jit(solution)/shard_map/reduce_scatter | solution.py:236
  1172.6 110.6 %reduce-scatter.11.cloned.1.call-done = bf16[512,1024]{1,0:T(8,128)(2,1)} async-done(((bf16[4096,1024]{1,0:T(8,128)(2,1)}), bf16[512,1024]{1,0:T(8,128)(2,1)}) %reduce-scatter.11.cloned.1.call-update) | async-done | bytes 1048592 | tf_op jit(solution)/shard_map/reduce_scatter | solution.py:243
  1288.6 37.8 %all-reduce.7 = (bf16[2048]{0:T(1024)(128)(2,1)S(1)}, bf16[1024]{0:T(1024)(128)(2,1)S(1)}, bf16[4096]{0:T(1024)(128)(2,1)S(1)}, bf16[1024]{0:T(1024)(128)(2,1)S(1)}, bf16[6144]{0:T(1024)(128)(2,1)S(1)}) all-reduce(bf16[2048]{0:T(1024)(128)(2,1)S(1)} %pad_maximum_fusion.1, ...), channel_id=6, replica_groups=mesh['rep'=16,'shard'=8] {'shard'}, use_global_device_ids=true, to_apply=%region_24.0.clone | all-reduce | flops 14336 | bytes 57344
  1326.8 27.6 %all-reduce.5 = (bf16[256]{0:T(256)(128)(2,1)S(1)}, bf16[128]{0:T(256)(128)(2,1)S(1)}, bf16[512]{0:T(512)(128)(2,1)S(1)}, bf16[128]{0:T(256)(128)(2,1)S(1)}, bf16[768]{0:T(1024)(128)(2,1)S(1)}) all-reduce(bf16[256]{0:T(256)(128)(2,1)S(1)} %dynamic-slice.1, ...), channel_id=1, replica_groups=mesh['rep'=16,'shard'=8] {'rep'}, use_global_device_ids=true, to_apply=%region_25.0 | all-reduce | flops 1792 | bytes 7168 | tf_op jit(solution)/shard_map/psum | solution.py:272
  1357.2 12.8 fusion.50
  1370.0 19.0 %psum.70 = f32[1,1024]{1,0:T(1,128)S(1)} all-reduce(f32[1,1024]{1,0:T(1,128)S(1)} %fusion.50), channel_id=1, replica_groups=mesh['rep'=16,'shard'=8] {'shard'}, use_global_device_ids=true, to_apply=%region_19.0 | all-reduce | flops 1024 | bytes 8192 | tf_op jit(solution)/shard_map/psum | solution.py:227
  1389.6 24.9 %all-reduce.10.cloned.1.call-done = (bf16[128,1024]{1,0:T(8,128)(2,1)}, bf16[128,4096]{1,0:T(8,128)(2,1)}, bf16[512,1024]{1,0:T(8,128)(2,1)}, bf16[128,6144]{1,0:T(8,128)(2,1)}) async-done(((bf16[128,1024]{1,0:T(8,128)(2,1)}, bf16[128,4096]{1,0:T(8,128)(2,1)}, bf16[512,1024]{1,0:T(8,128)(2,1)}, bf16[128,6144]{1,0:T(8,128)(2,1)}), (bf16[128,1024]{1,0:T(8,128)(2,1)}, bf16[128,4096]{1,0:T(8,128)(2,1)}, ...) | async-done | bytes 3932176 | tf_op jit(solution)/shard_map/psum | solution.py:273
  1422.8 66.0 %all-gather.29.cloned.1.call-done = bf16[2048,3072]{1,0:T(8,128)(2,1)} async-done(((bf16[128,3072]{1,0:T(8,128)(2,1)}), bf16[2048,3072]{1,0:T(8,128)(2,1)}) %all-gather.29.cloned.1.call-update) | async-done | bytes 12582928 | tf_op jit(solution)/shard_map/all_gather | solution.py:271
  1488.7 7.4 reduce_sum.266
  (172 shorter events, 120.9 us)
Async XLA Ops:
  7.2 150.7 %all-gather.15.cloned.1.call-start = ((), (), s32[]{:S(2)}) async-start(), calls=%async_computation.4 | async-start | bytes 14155776 | tf_op jit(solution)/shard_map/all_gather | solution.py:70
  7.9 239.0 %all-gather.17.cloned.1.call-start = ((), (), s32[]{:S(2)}) async-start(), calls=%async_computation.5 | async-start | bytes 7077888 | tf_op jit(solution)/shard_map/all_gather | solution.py:62
  8.7 295.1 %all-gather.19.cloned.1.call-start = ((), (), s32[]{:S(2)}) async-start(), calls=%async_computation.6 | async-start | bytes 2359296 | tf_op jit(solution)/shard_map/all_gather | solution.py:97
  70.0 176.9 %copy-start.3 = (bf16[1,128,1024]{2,1,0:T(8,128)(2,1)S(1)}, bf16[1,128,1024]{2,1,0:T(8,128)(2,1)}, u32[]{:S(2)}) copy-start(bf16[1,128,1024]{2,1,0:T(8,128)(2,1)} %param.13) | copy-start | bytes 786436
  251.6 106.7 %all-gather.21.cloned.1.call-start = ((), (), s32[]{:S(2)}) async-start(), calls=%async_computation.7 | async-start | bytes 2359296 | tf_op jit(solution)/shard_map/all_gather | solution.py:96
  252.5 159.9 %all-gather.23.cloned.1.call-start = ((), (), s32[]{:S(2)}) async-start(), calls=%async_computation.8 | async-start | bytes 2359296 | tf_op jit(solution)/shard_map/all_gather | solution.py:64
  253.1 266.4 %all-gather.25.cloned.1.call-start = ((), (), s32[]{:S(2)}) async-start(), calls=%async_computation.9 | async-start | bytes 9437184 | tf_op jit(solution)/shard_map/all_gather | solution.py:66
  253.6 373.1 %all-gather.27.cloned.1.call-start = ((), (), s32[]{:S(2)}) async-start(), calls=%async_computation.10 | async-start | bytes 9437184 | tf_op jit(solution)/shard_map/all_gather | solution.py:68
  254.4 483.8 %reduce-scatter.15.cloned.1.call-start = ((), (), s32[]{:S(2)}) async-start(), calls=%async_computation.15 | async-start | bytes 2359296
  303.2 58.0 %copy-start.10 = (bf16[1,128,1024]{1,2,0:T(8,128)(2,1)}, bf16[1,128,1024]{1,2,0:T(8,128)(2,1)S(1)}, u32[]{:S(2)}) copy-start(bf16[1,128,1024]{1,2,0:T(8,128)(2,1)S(1)} %copy.41) | copy-start | bytes 786436
  368.6 150.8 %copy-start.23 = (bf16[16,64,128]{2,1,0:T(8,128)(2,1)}, bf16[16,64,128]{2,1,0:T(8,128)(2,1)S(1)}, u32[]{:S(2)}) copy-start(bf16[16,64,128]{2,1,0:T(8,128)(2,1)S(1)} %fusion.16) | copy-start | bytes 786436
  519.5 107.3 %copy-start.16 = (bf16[1,128,1024]{2,1,0:T(8,128)(2,1)S(1)}, bf16[1,128,1024]{2,1,0:T(8,128)(2,1)}, u32[]{:S(2)}) copy-start(bf16[1,128,1024]{2,1,0:T(8,128)(2,1)} %param.15) | copy-start | bytes 786436
  626.7 8.3 copy-start.1
  635.0 4.1 copy-start.17
  635.0 5.0 copy-start.6
  665.3 150.9 %reduce-scatter.13.cloned.1.call-start = ((), (), s32[]{:S(2)}) async-start(), calls=%async_computation.14 | async-start | bytes 2359296
  672.4 6.6 copy-start.11
  691.9 4.5 copy-start.24
  691.9 4.5 copy-start.27
  696.4 469.6 %reduce-scatter.9.cloned.1.call-start = ((), (), s32[]{:S(2)}) async-start(), calls=%async_computation.11 | async-start | bytes 33030144 | tf_op jit(solution)/shard_map/reduce_scatter | solution.py:236
  722.3 4.1 copy-start.9
  726.4 91.9 %copy-start.20 = (bf16[16,64,128]{2,1,0:T(8,128)(2,1)}, bf16[16,64,128]{2,1,0:T(8,128)(2,1)S(1)}, u32[]{:S(2)}) copy-start(bf16[16,64,128]{2,1,0:T(8,128)(2,1)S(1)} %get-tuple-element.63) | copy-start | bytes 786436
  740.2 78.1 %copy-start.21 = (bf16[1,128,1024]{1,2,0:T(8,128)(2,1)}, bf16[1,128,1024]{1,2,0:T(8,128)(2,1)S(1)}, u32[]{:S(2)}) copy-start(bf16[1,128,1024]{1,2,0:T(8,128)(2,1)S(1)} %copy.48) | copy-start | bytes 786436
  823.6 8.7 copy-start.4
  823.6 8.7 copy-start.14
  838.6 7.5 copy-start.5
  865.1 418.1 %reduce-scatter.11.cloned.1.call-start = ((), (), s32[]{:S(2)}) async-start(), calls=%async_computation.12 | async-start | bytes 9437184 | tf_op jit(solution)/shard_map/reduce_scatter | solution.py:243
  871.6 542.9 %all-reduce.10.cloned.1.call-start = ((), (), s32[]{:S(2)}) async-start(), calls=%async_computation.16 | async-start | bytes 7864320 | tf_op jit(solution)/shard_map/psum | solution.py:273
  1169.9 115.5 %copy-start.28 = (u32[128]{0:T(128)S(1)}, u32[128]{0:T(128)}, u32[]{:S(2)}) copy-start(u32[128]{0:T(128)} %constant.44) | copy-start | bytes 1540
  1283.2 205.5 %all-gather.29.cloned.1.call-start = ((), (), s32[]{:S(2)}) async-start(), calls=%async_computation.13 | async-start | bytes 13369344 | tf_op jit(solution)/shard_map/all_gather | solution.py:271
  1414.5 4.7 copy-start.19
  1414.5 6.3 copy-start.15
  (10 other events, 22.6 us)
Sparse Core Ops, SparseCore 0:
  10.3 147.5 all-gather.14
  160.2 86.6 all-gather.16
  251.8 51.9 all-gather.18
  306.5 51.7 all-gather.20
  360.5 51.7 all-gather.22
  414.6 104.8 all-gather.24
  521.8 104.8 all-gather.26
  665.4 72.7 reduce-scatter.14
  742.5 73.6 reduce-scatter.12
  865.2 300.6 reduce-scatter.8
  1169.7 113.4 reduce-scatter.10
  1287.2 127.2 all-reduce.9
  1416.2 72.4 all-gather.28
